TPU v7x, 32 devices: a whole 2x2x4 slice. The times are simulated.
32 devices in a mesh: groups: 2 (over x), row: 16 (over z, y, core).
Axes of the slice: x: 2, y: 2, z: 4, core: 2. Of those that a mesh axis runs over, the one named last changes fastest.
Arguments:
- positions: float32 [8, 512, 2048], P(None, ('groups', 'row')), parts along dimension 1, may hold values from -3 to 3
- momenta: float32 [8, 512, 2048], P(None, ('groups', 'row')), parts along dimension 1, may hold values from -5 to 5
- step_size: float32 [16], P('groups'), parts along dimension 0, may hold values from 0.1 to 0.3
- counts: float32 [512, 2048], P(('groups', 'row')), parts along dimension 0, may hold values from 0 to 3
- exposure: float32 [512, 2048], P(('groups', 'row')), parts along dimension 0, may hold values from 0.05 to 0.5
- precision_diag: float32 [512, 2048], P(('groups', 'row')), parts along dimension 0, may hold values from 0.5 to 4
- kind_blocks: float32 [4, 128, 128], replicated, as said below
- vertical_coupling: float32 [128, 128], replicated, may hold values from -0.5 to 0.5
- matched_coupling: float32 [128, 128], replicated, as said below
- partner: int32 [8192], P(('groups', 'row')), parts along dimension 0, may hold values from 0 to 4095, as said below
- block_kind: int32 [512, 16], P(('groups', 'row')), parts along dimension 0, may hold values from 0 to 3
Outputs:
- new_positions: float32 [8, 512, 2048], P(None, ('groups', 'row')), parts along dimension 1
- new_momenta: float32 [8, 512, 2048], P(None, ('groups', 'row')), parts along dimension 1
There are 2 independent parts, one for each index of `groups`. A program takes and returns all parts, laid end to end along the dimension named above; an argument that names none is the same for every part. Nothing has to cross between parts.
Inputs may be any that keep to these rules, and one draw needn't show every extreme that they name: partner pairs the blocks: partner[partner[b]] = b and partner[b] != b; the 256 blocks of each index of row have exactly 16 partners among the blocks of every index of row, their own included. `kind_blocks`: each matrix is symmetric. `matched_coupling`: symmetric.
All inputs are finite; a program needn't handle non-finite values.
Results may differ from a plain program's by a relative error of at most 0.0001.
Values sent between devices are 32-bit elements; how exact they have to be, the bound alone decides.
A program may use at most 64 MiB of HBM per device.

v0:
```python
import jax
import jax.numpy as jnp
from jax import lax
from jax.sharding import PartitionSpec as P

highest = lax.Precision.HIGHEST


def padded_2(cells, sides, width):
    for axis, dim in sides:
        count = lax.axis_size(axis)
        ends = count - 1
        head = lax.slice_in_dim(cells, 0, width, axis=dim)
        tail = lax.slice_in_dim(cells, cells.shape[dim] - width, cells.shape[dim], axis=dim)
        cells = jnp.concatenate(
            [
                lax.ppermute(tail, axis, [(i, (i + 1) % count) for i in range(ends)]),
                cells,
                lax.ppermute(head, axis, [((i + 1) % count, i) for i in range(ends)]),
            ],
            axis=dim,
        )
    return cells


def routing_tables(partner):
    block_count = partner.shape[0]
    devices = lax.axis_size("row")
    pair_count = block_count // devices
    target = partner // block_count
    remote = partner % block_count
    local_ids = jnp.arange(block_count, dtype=jnp.int32)
    same_target = target[:, None] == target[None, :]
    send_rank = jnp.sum(same_target & (local_ids[None, :] < local_ids[:, None]), axis=1)
    recv_rank = jnp.sum(same_target & (remote[None, :] < remote[:, None]), axis=1)
    send_order = (
        jnp.zeros((block_count,), jnp.int32).at[target * pair_count + send_rank].set(local_ids)
    )
    return (send_order, target * pair_count + recv_rank, pair_count)


def potential_grad(
    current,
    tables,
    counts,
    exposure,
    precision_diag,
    kind_blocks,
    vertical_coupling,
    matched_coupling,
    block_kind,
):
    send_order, recv_pos, pair_count = tables
    chains, strip_rows, grid_cols = current.shape
    kinds = kind_blocks.shape[0]
    block_width = kind_blocks.shape[1]
    per_row = grid_cols // block_width
    flat_blocks = current.reshape(chains, strip_rows * per_row, block_width)
    outgoing = jnp.take(flat_blocks, send_order, axis=1)
    mapped = jnp.einsum(
        "cbk,kl->cbl",
        lax.all_to_all(outgoing, "row", split_axis=1, concat_axis=1, tiled=True),
        matched_coupling,
        precision=highest,
    )
    padded = padded_2(current, (("row", 1),), 1)
    blocks = current.reshape(chains, strip_rows, per_row, block_width)
    all_kinds = jnp.einsum("crnk,qkl->qcrnl", blocks, kind_blocks, precision=highest)
    kind_mask = (block_kind[None] == jnp.arange(kinds, dtype=jnp.int32)[:, None, None]).astype(
        jnp.float32
    )
    within = jnp.sum(all_kinds * kind_mask[:, None, :, :, None], axis=0)
    upper_rows = padded[:, :-2].reshape(chains, strip_rows, per_row, block_width)
    lower_rows = padded[:, 2:].reshape(chains, strip_rows, per_row, block_width)
    vertical = jnp.einsum("crnk,lk->crnl", lower_rows, vertical_coupling, precision=highest)
    vertical = vertical + jnp.einsum(
        "crnk,kl->crnl", upper_rows, vertical_coupling, precision=highest
    )
    matched = jnp.take(mapped, recv_pos, axis=1).reshape(chains, strip_rows, per_row, block_width)
    coupled = (within - vertical - matched).reshape(chains, strip_rows, grid_cols)
    return (
        coupled + precision_diag[None] * current - counts[None] + exposure[None] * jnp.exp(current)
    )


def body(
    positions,
    momenta,
    step_size,
    counts,
    exposure,
    precision_diag,
    kind_blocks,
    vertical_coupling,
    matched_coupling,
    partner,
    block_kind,
):
    tables = routing_tables(partner)
    step_len = step_size[:, None, None]

    def gradient_at(current):
        return potential_grad(
            current,
            tables,
            counts,
            exposure,
            precision_diag,
            kind_blocks,
            vertical_coupling,
            matched_coupling,
            block_kind,
        )

    half_step = momenta - 0.5 * step_len * gradient_at(positions)
    moved_once = positions + step_len * half_step
    full_step = half_step - step_len * gradient_at(moved_once)
    new_positions = moved_once + step_len * full_step
    new_momenta = full_step - 0.5 * step_len * gradient_at(new_positions)
    return (new_positions, new_momenta)


def solution(mesh):
    return jax.shard_map(
        body,
        mesh=mesh,
        in_specs=(
            P(None, ("groups", "row"), None),
            P(None, ("groups", "row"), None),
            P("groups"),
            P(("groups", "row"), None),
            P(("groups", "row"), None),
            P(("groups", "row"), None),
            P(),
            P(),
            P(),
            P(("groups", "row")),
            P(("groups", "row"), None),
        ),
        out_specs=(P(None, ("groups", "row"), None), P(None, ("groups", "row"), None)),
        check_vma=False,
    )
```

profile of v0, /device:TPU:15, one launch (start us, length us, event | category | flops | bytes accessed | tf_op | source)
XLA Modules:
  0.0 162.0 jit_solution(6844901424366116784)
XLA Ops:
  7.5 6.7 %all-to-all-start = ((f32[8,256,128]{2,0,1:T(8,128)}), f32[8,256,128]{2,0,1:T(8,128)S(1)}, u32[]{:S(2)}, u32[]{:S(2)}) async-start(f32[8,256,128]{2,0,1:T(8,128)} %select_bitcast_fusion.5), calls=%async_computation | async-start | bytes 2097152 | tf_op jit(solution)/shard_map/all_to_all | solution.py:62
  14.3 3.3 %collective-permute-start.1 = (f32[8,1,2048]{2,1,0:T(1,128)S(1)}, f32[8,1,2048]{2,1,0:T(1,128)S(1)}, u32[]{:S(2)}, u32[]{:S(2)}) collective-permute-start(f32[8,1,2048]{2,1,0:T(1,128)S(1)} %get-tuple-element.19), channel_id=1, source_target_pairs={{0,1},{1,2},{2,3},{3,4},{4,5},{5,6},{6,7},{7,8},{8,9},{9,10},{10,1... | collective-permute-start | bytes 196616 | tf_op jit(solution)/shard_map/ppermute | solution.py:17
  17.6 2.1 %collective-permute-start = (f32[8,1,2048]{2,1,0:T(1,128)S(1)}, f32[8,1,2048]{2,1,0:T(1,128)S(1)}, u32[]{:S(2)}, u32[]{:S(2)}) collective-permute-start(f32[8,1,2048]{2,1,0:T(1,128)S(1)} %get-tuple-element.20), channel_id=1, source_target_pairs={{1,0},{2,1},{3,2},{4,3},{5,4},{6,5},{7,6},{8,7},{9,8},{10,9},{11,1... | collective-permute-start | bytes 196616 | tf_op jit(solution)/shard_map/ppermute | solution.py:19
  20.4 3.8 %multiply_reduce_fusion = f32[128,8,16,16]{0,3,2,1:T(8,128)S(1)} fusion(f32[8,16,16,128,1]{3,2,1,0,4:T(8,128)S(1)} %bitcast.147, f32[4,16,16]{2,1,0:T(8,128)S(1)} %fusion.34, f32[4,128,128]{2,1,0:T(8,128)S(1)} %copy-done), kind=kOutput, calls=%fused_computation.11 | convolution fusion | flops 1612447744 | bytes 2363392 | tf_op jit(solution)/shard_map/crnk,qkl->qcrnl/dot_general | solution.py:68
  24.8 13.2 %collective-permute-done.1 = f32[8,1,2048]{2,1,0:T(1,128)S(1)} collective-permute-done((f32[8,1,2048]{2,1,0:T(1,128)S(1)}, f32[8,1,2048]{2,1,0:T(1,128)S(1)}, u32[]{:S(2)}, u32[]{:S(2)}) %collective-permute-start.1) | collective-permute-done | bytes 65568 | tf_op jit(solution)/shard_map/ppermute | solution.py:17
  42.1 2.0 %fusion.15 = f32[8,16,16,128]{3,2,1,0:T(8,128)} fusion(f32[128,128]{1,0:T(8,128)S(1)} %copy-done.11, f32[8,16,16,128]{3,2,1,0:T(8,128)S(1)} %bitcast.150), kind=kOutput, calls=%fused_computation.28 | convolution fusion | flops 402653184 | bytes 2162688 | tf_op jit(solution)/shard_map/crnk,lk->crnl/dot_general | solution.py:75
  44.0 1.9 %fusion.26 = f32[8,256,128]{2,0,1:T(8,128)} fusion(f32[8,256,128]{2,0,1:T(8,128)S(1)} %all-to-all-done, f32[128,128]{1,0:T(8,128)S(1)} %copy-done.13), kind=kOutput, calls=%fused_computation.61 | convolution fusion | flops 402653184 | bytes 2162688 | tf_op jit(solution)/shard_map/cbk,kl->cbl/dot_general | solution.py:60
  46.0 2.0 %gather_fusion.1 = f32[256,8,128]{2,1,0:T(8,128)S(1)} fusion(f32[8,256,128]{2,0,1:T(8,128)} %fusion.26, s32[1024]{0:T(1024)S(1)} %pad_clamp_fusion), kind=kCustom, calls=%fused_computation.1.clone | custom fusion | bytes 2098176 | tf_op jit(solution)/shard_map/jit(_take)/gather | solution.py:79
  51.9 3.1 %multiply_add_fusion.1 = (f32[8,16,2048]{2,1,0:T(8,128)S(1)}, f32[8,16,2048]{2,1,0:T(8,128)}) fusion(f32[8,16,2048]{2,1,0:T(8,128)S(1)} %copy-done.1, f32[8]{0:T(128)S(1)} %copy-done.18, f32[8,16,2048]{2,1,0:T(8,128)} %param.14, f32[16,2048]{1,0:T(8,128)} %param.17, f32[16,2048]{1,0:T(8,128)} %param.16, f32[8,16,2048]{2,1,0:T(8,128)} %reshape.83, ...), kind=kLoop, calls=%fused_computation.47 | loop fusion | flops 2359296 | bytes 5636160 | tf_op jit(solution)/shard_map/add | solution.py:116
  56.8 2.0 %gather_fusion.2 = f32[256,8,128]{2,1,0:T(8,128)S(1)} fusion(f32[8,256,128]{2,0,1:T(8,128)} %copy.55, s32[1024]{0:T(1024)S(1)} %pad_clamp_fusion.1), kind=kCustom, calls=%fused_computation.2.clone | custom fusion | bytes 2098176 | tf_op jit(solution)/shard_map/jit(_take)/gather | solution.py:59
  58.8 2.0 %select_bitcast_fusion.3 = f32[8,256,128]{2,0,1:T(8,128)} fusion(f32[256,8,128]{2,1,0:T(8,128)S(1)} %gather_fusion.2, pred[256]{0:T(512)(128)(4,1)} %copy-done.19), kind=kLoop, calls=%fused_computation.41 | loop fusion | flops 262144 | bytes 2097408 | tf_op jit(solution)/shard_map/jit(_take)/select_n | solution.py:59
  60.7 4.6 %all-to-all-start.1 = ((f32[8,256,128]{2,0,1:T(8,128)}), f32[8,256,128]{2,0,1:T(8,128)S(1)}, u32[]{:S(2)}, u32[]{:S(2)}) async-start(f32[8,256,128]{2,0,1:T(8,128)} %select_bitcast_fusion.3), calls=%async_computation.1 | async-start | bytes 2097152 | tf_op jit(solution)/shard_map/all_to_all | solution.py:62
  66.2 3.3 %collective-permute-start.3 = (f32[8,1,2048]{2,1,0:T(1,128)S(1)}, f32[8,1,2048]{2,1,0:T(1,128)S(1)}, u32[]{:S(2)}, u32[]{:S(2)}) collective-permute-start(f32[8,1,2048]{2,1,0:T(1,128)S(1)} %get-tuple-element.15), channel_id=1, source_target_pairs={{0,1},{1,2},{2,3},{3,4},{4,5},{5,6},{6,7},{7,8},{8,9},{9,10},{10,1... | collective-permute-start | bytes 196616 | tf_op jit(solution)/shard_map/ppermute | solution.py:17
  69.5 2.1 %collective-permute-start.2 = (f32[8,1,2048]{2,1,0:T(1,128)S(1)}, f32[8,1,2048]{2,1,0:T(1,128)S(1)}, u32[]{:S(2)}, u32[]{:S(2)}) collective-permute-start(f32[8,1,2048]{2,1,0:T(1,128)S(1)} %get-tuple-element.16), channel_id=1, source_target_pairs={{1,0},{2,1},{3,2},{4,3},{5,4},{6,5},{7,6},{8,7},{9,8},{10,9},{11,1... | collective-permute-start | bytes 196616 | tf_op jit(solution)/shard_map/ppermute | solution.py:19
  71.9 4.8 %fusion.1 = f32[8,16,16,128]{3,2,1,0:T(8,128)} fusion(f32[4,16,16]{2,0,1:T(4,128)S(1)} %copy.54, f32[8,16,16,128,1]{3,2,1,0,4:T(8,128)S(1)} %bitcast.149, f32[4,128,128]{2,1,0:T(8,128)S(1)} %copy-done), kind=kOutput, calls=%fused_computation.10 | convolution fusion | flops 1612447744 | bytes 2363392 | tf_op jit(solution)/shard_map/crnk,qkl->qcrnl/dot_general | solution.py:68
  76.7 12.5 %collective-permute-done.3 = f32[8,1,2048]{2,1,0:T(1,128)S(1)} collective-permute-done((f32[8,1,2048]{2,1,0:T(1,128)S(1)}, f32[8,1,2048]{2,1,0:T(1,128)S(1)}, u32[]{:S(2)}, u32[]{:S(2)}) %collective-permute-start.3) | collective-permute-done | bytes 65568 | tf_op jit(solution)/shard_map/ppermute | solution.py:17
  92.5 2.0 %fusion.12 = f32[8,16,16,128]{3,2,1,0:T(8,128)} fusion(f32[128,128]{1,0:T(8,128)S(1)} %copy-done.11, f32[8,16,16,128]{3,2,1,0:T(8,128)S(1)} %bitcast.151), kind=kOutput, calls=%fused_computation.25 | convolution fusion | flops 402653184 | bytes 2162688 | tf_op jit(solution)/shard_map/crnk,lk->crnl/dot_general | solution.py:75
  99.6 1.8 %multiply_add_fusion = f32[8,16,2048]{2,1,0:T(8,128)S(1)} fusion(f32[8]{0:T(128)S(1)} %copy-done.18, f32[8,16,2048]{2,1,0:T(8,128)} %get-tuple-element.6, f32[16,2048]{1,0:T(8,128)} %param.17, f32[16,2048]{1,0:T(8,128)} %param.16, f32[8,16,2048]{2,1,0:T(8,128)S(1)} %reshape.89, f32[16,2048]{1,0:T(8,128)} %param.18, f32[8,16,2048]{2,1,0:T(8,128)S(1)} %copy-done.1), kind=kLoop, calls=%fused_computation.45 | loop fusion | flops 2883584 | bytes 4587552 | tf_op jit(solution)/shard_map/add | solution.py:118
  102.7 2.9 %copy.59 = f32[8,256,128]{2,0,1:T(8,128)} copy(f32[8,256,128]{2,1,0:T(8,128)} %reshape.93) | data formatting | bytes 2097152 | tf_op jit(solution)/shard_map/reshape | solution.py:58
  105.6 3.0 %gather_fusion.4 = f32[256,8,128]{2,1,0:T(8,128)} fusion(f32[8,256,128]{2,0,1:T(8,128)} %copy.59, s32[1024]{0:T(1024)S(1)} %pad_clamp_fusion.1), kind=kCustom, calls=%fused_computation.4.clone | custom fusion | bytes 2098176 | tf_op jit(solution)/shard_map/jit(_take)/gather | solution.py:59
  108.6 2.6 %select_bitcast_fusion.1 = f32[8,256,128]{2,0,1:T(8,128)} fusion(f32[256,8,128]{2,1,0:T(8,128)} %gather_fusion.4, pred[256]{0:T(512)(128)(4,1)} %copy-done.19), kind=kLoop, calls=%fused_computation.39 | loop fusion | flops 262144 | bytes 2097408 | tf_op jit(solution)/shard_map/jit(_take)/select_n | solution.py:59
  111.2 4.5 %all-to-all-start.2 = ((f32[8,256,128]{2,0,1:T(8,128)}), f32[8,256,128]{2,0,1:T(8,128)}, u32[]{:S(2)}, u32[]{:S(2)}) async-start(f32[8,256,128]{2,0,1:T(8,128)} %select_bitcast_fusion.1), calls=%async_computation.2 | async-start | bytes 2097152 | tf_op jit(solution)/shard_map/all_to_all | solution.py:62
  115.8 3.4 %collective-permute-start.5 = (f32[8,1,2048]{2,1,0:T(1,128)S(1)}, f32[8,1,2048]{2,1,0:T(1,128)S(1)}, u32[]{:S(2)}, u32[]{:S(2)}) collective-permute-start(f32[8,1,2048]{2,1,0:T(1,128)S(1)} %get-tuple-element.11), channel_id=1, source_target_pairs={{0,1},{1,2},{2,3},{3,4},{4,5},{5,6},{6,7},{7,8},{8,9},{9,10},{10,1... | collective-permute-start | bytes 196616 | tf_op jit(solution)/shard_map/ppermute | solution.py:17
  119.2 2.2 %collective-permute-start.4 = (f32[8,1,2048]{2,1,0:T(1,128)S(1)}, f32[8,1,2048]{2,1,0:T(1,128)S(1)}, u32[]{:S(2)}, u32[]{:S(2)}) collective-permute-start(f32[8,1,2048]{2,1,0:T(1,128)S(1)} %get-tuple-element.12), channel_id=1, source_target_pairs={{1,0},{2,1},{3,2},{4,3},{5,4},{6,5},{7,6},{8,7},{9,8},{10,9},{11,1... | collective-permute-start | bytes 196616 | tf_op jit(solution)/shard_map/ppermute | solution.py:19
  122.1 4.8 %fusion = f32[8,16,16,128]{3,2,1,0:T(8,128)} fusion(f32[4,16,16]{2,0,1:T(4,128)S(1)} %copy-done.15, f32[8,16,16,128,1]{3,2,1,0,4:T(8,128)S(1)} %bitcast.148, f32[4,128,128]{2,1,0:T(8,128)S(1)} %copy-done), kind=kOutput, calls=%fused_computation.8 | convolution fusion | flops 1612447744 | bytes 2363392 | tf_op jit(solution)/shard_map/crnk,qkl->qcrnl/dot_general | solution.py:68
  126.9 12.7 %collective-permute-done.5 = f32[8,1,2048]{2,1,0:T(1,128)S(1)} collective-permute-done((f32[8,1,2048]{2,1,0:T(1,128)S(1)}, f32[8,1,2048]{2,1,0:T(1,128)S(1)}, u32[]{:S(2)}, u32[]{:S(2)}) %collective-permute-start.5) | collective-permute-done | bytes 65568 | tf_op jit(solution)/shard_map/ppermute | solution.py:17
  142.9 1.9 %fusion.9 = f32[8,16,16,128]{3,2,1,0:T(8,128)} fusion(f32[128,128]{1,0:T(8,128)S(1)} %copy-done.11, f32[8,16,16,128]{3,2,1,0:T(8,128)S(1)} %bitcast.152), kind=kOutput, calls=%fused_computation.22 | convolution fusion | flops 402653184 | bytes 2162688 | tf_op jit(solution)/shard_map/crnk,lk->crnl/dot_general | solution.py:75
  144.8 3.2 %fusion.22 = f32[8,256,128]{2,0,1:T(8,128)} fusion(f32[8,256,128]{2,0,1:T(8,128)} %all-to-all-done.2, f32[128,128]{1,0:T(8,128)S(1)} %copy-done.13), kind=kOutput, calls=%fused_computation.57 | convolution fusion | flops 402653184 | bytes 2162688 | tf_op jit(solution)/shard_map/cbk,kl->cbl/dot_general | solution.py:60
  148.1 3.0 %gather_fusion.5 = f32[256,8,128]{2,1,0:T(8,128)} fusion(f32[8,256,128]{2,0,1:T(8,128)} %fusion.22, s32[1024]{0:T(1024)S(1)} %pad_clamp_fusion), kind=kCustom, calls=%fused_computation.5.clone | custom fusion | bytes 2098176 | tf_op jit(solution)/shard_map/jit(_take)/gather | solution.py:79
  154.2 1.9 %fusion.7 = f32[8,16,16,128]{3,2,1,0:T(8,128)} fusion(f32[8,16,16,128]{3,2,1,0:T(8,128)S(1)} %bitcast.158, f32[8,16,16,128]{3,2,1,0:T(8,128)S(1)} %copy-done.3, f32[8,16,16,128]{3,2,1,0:T(8,128)S(1)} %copy-done.8, f32[128,128]{1,0:T(8,128)S(1)} %copy-done.11, f32[8,16,16,128]{3,2,1,0:T(8,128)S(1)} %bitcast.153), kind=kOutput, calls=%fused_computation.20 | convolution fusion | flops 403439616 | bytes 5308416 | tf_op jit(solution)/shard_map/crnk,kl->crnl/dot_general | solution.py:76
  156.2 2.4 %reshape.95 = f32[8,16,2048]{2,1,0:T(8,128)} reshape(f32[8,16,16,128]{3,2,1,0:T(8,128)} %fusion.7) | data formatting | bytes 2097152 | tf_op jit(solution)/shard_map/reshape | solution.py:80
  158.6 3.4 %multiply_subtract_fusion = f32[8,16,2048]{2,1,0:T(8,128)} fusion(f32[8,16,2048]{2,1,0:T(8,128)S(1)} %multiply_add_fusion, f32[8,16,2048]{2,1,0:T(8,128)} %reshape.95, f32[16,2048]{1,0:T(8,128)S(1)} %copy-done.12, f32[16,2048]{1,0:T(8,128)} %param.16, f32[16,2048]{1,0:T(8,128)} %param.18, f32[8]{0:T(128)S(1)} %copy-done.20, ...), kind=kLoop, calls=%fused_computation.44 | loop fusion | flops 4194304 | bytes 6684736 | tf_op jit(solution)/shard_map/sub | solution.py:119
  (95 shorter events, 35.7 us)
Async XLA Ops:
  0.6 19.8 %copy-start = (f32[4,128,128]{2,1,0:T(8,128)S(1)}, f32[4,128,128]{2,1,0:T(8,128)}, u32[]{:S(2)}) copy-start(f32[4,128,128]{2,1,0:T(8,128)} %param.19) | copy-start | bytes 786436
  3.1 3.1 %copy-start.19 = (pred[256]{0:T(512)(128)(4,1)}, pred[256]{0:T(512)(128)(4,1)S(1)}, u32[]{:S(2)}) copy-start(pred[256]{0:T(512)(128)(4,1)S(1)} %compare_and_fusion.3) | copy-start | bytes 772
  7.5 6.7 %copy-start.1 = (f32[8,16,2048]{2,1,0:T(8,128)S(1)}, f32[8,16,2048]{2,1,0:T(8,128)}, u32[]{:S(2)}) copy-start(f32[8,16,2048]{2,1,0:T(8,128)} %param.13) | copy-start | bytes 3145732
  7.5 36.6 %all-to-all-start = ((f32[8,256,128]{2,0,1:T(8,128)}), f32[8,256,128]{2,0,1:T(8,128)S(1)}, u32[]{:S(2)}, u32[]{:S(2)}) async-start(f32[8,256,128]{2,0,1:T(8,128)} %select_bitcast_fusion.5), calls=%async_computation | async-start | bytes 2097152 | tf_op jit(solution)/shard_map/all_to_all | solution.py:62
  14.3 23.8 %collective-permute-start.1 = (f32[8,1,2048]{2,1,0:T(1,128)S(1)}, f32[8,1,2048]{2,1,0:T(1,128)S(1)}, u32[]{:S(2)}, u32[]{:S(2)}) collective-permute-start(f32[8,1,2048]{2,1,0:T(1,128)S(1)} %get-tuple-element.19), channel_id=1, source_target_pairs={{0,1},{1,2},{2,3},{3,4},{4,5},{5,6},{6,7},{7,8},{8,9},{9,10},{10,1... | collective-permute-start | bytes 196616 | tf_op jit(solution)/shard_map/ppermute | solution.py:17
  17.6 22.1 %collective-permute-start = (f32[8,1,2048]{2,1,0:T(1,128)S(1)}, f32[8,1,2048]{2,1,0:T(1,128)S(1)}, u32[]{:S(2)}, u32[]{:S(2)}) collective-permute-start(f32[8,1,2048]{2,1,0:T(1,128)S(1)} %get-tuple-element.20), channel_id=1, source_target_pairs={{1,0},{2,1},{3,2},{4,3},{5,4},{6,5},{7,6},{8,7},{9,8},{10,9},{11,1... | collective-permute-start | bytes 196616 | tf_op jit(solution)/shard_map/ppermute | solution.py:19
  19.7 0.7 copy-start.17
  20.4 3.9 %copy-start.16 = (f32[4,16,16]{2,1,0:T(8,128)}, f32[4,16,16]{2,1,0:T(8,128)S(1)}, u32[]{:S(2)}) copy-start(f32[4,16,16]{2,1,0:T(8,128)S(1)} %fusion.34) | copy-start | bytes 12292
  20.4 3.9 %copy-start.18 = (f32[8]{0:T(128)S(1)}, f32[8]{0:T(128)}, u32[]{:S(2)}) copy-start(f32[8]{0:T(128)} %param.15) | copy-start | bytes 100
  41.2 0.8 copy-start.11
  42.1 2.0 %copy-start.13 = (f32[128,128]{1,0:T(8,128)S(1)}, f32[128,128]{1,0:T(8,128)}, u32[]{:S(2)}) copy-start(f32[128,128]{1,0:T(8,128)} %param.21) | copy-start | bytes 196612
  48.3 1.2 copy-start.6
  48.3 1.5 copy-start.9
  60.7 33.7 %all-to-all-start.1 = ((f32[8,256,128]{2,0,1:T(8,128)}), f32[8,256,128]{2,0,1:T(8,128)S(1)}, u32[]{:S(2)}, u32[]{:S(2)}) async-start(f32[8,256,128]{2,0,1:T(8,128)} %select_bitcast_fusion.3), calls=%async_computation.1 | async-start | bytes 2097152 | tf_op jit(solution)/shard_map/all_to_all | solution.py:62
  66.1 5.8 %copy-start.14 = (f32[4,16,16]{2,0,1:T(4,128)}, f32[4,16,16]{2,0,1:T(4,128)S(1)}, u32[]{:S(2)}) copy-start(f32[4,16,16]{2,0,1:T(4,128)S(1)} %copy.54) | copy-start | bytes 12292
  66.2 23.0 %collective-permute-start.3 = (f32[8,1,2048]{2,1,0:T(1,128)S(1)}, f32[8,1,2048]{2,1,0:T(1,128)S(1)}, u32[]{:S(2)}, u32[]{:S(2)}) collective-permute-start(f32[8,1,2048]{2,1,0:T(1,128)S(1)} %get-tuple-element.15), channel_id=1, source_target_pairs={{0,1},{1,2},{2,3},{3,4},{4,5},{5,6},{6,7},{7,8},{8,9},{9,10},{10,1... | collective-permute-start | bytes 196616 | tf_op jit(solution)/shard_map/ppermute | solution.py:17
  69.5 21.3 %collective-permute-start.2 = (f32[8,1,2048]{2,1,0:T(1,128)S(1)}, f32[8,1,2048]{2,1,0:T(1,128)S(1)}, u32[]{:S(2)}, u32[]{:S(2)}) collective-permute-start(f32[8,1,2048]{2,1,0:T(1,128)S(1)} %get-tuple-element.16), channel_id=1, source_target_pairs={{1,0},{2,1},{3,2},{4,3},{5,4},{6,5},{7,6},{8,7},{9,8},{10,9},{11,1... | collective-permute-start | bytes 196616 | tf_op jit(solution)/shard_map/ppermute | solution.py:19
  96.5 1.2 copy-start.10
  96.8 1.3 copy-start.4
  96.8 1.6 copy-start.7
  101.4 57.1 %copy-start.2 = (f32[8,16,2048]{2,1,0:T(8,128)}, f32[8,16,2048]{2,1,0:T(8,128)S(1)}, u32[]{:S(2)}) copy-start(f32[8,16,2048]{2,1,0:T(8,128)S(1)} %multiply_add_fusion) | copy-start | bytes 3145732
  111.2 33.7 %all-to-all-start.2 = ((f32[8,256,128]{2,0,1:T(8,128)}), f32[8,256,128]{2,0,1:T(8,128)}, u32[]{:S(2)}, u32[]{:S(2)}) async-start(f32[8,256,128]{2,0,1:T(8,128)} %select_bitcast_fusion.1), calls=%async_computation.2 | async-start | bytes 2097152 | tf_op jit(solution)/shard_map/all_to_all | solution.py:62
  115.8 23.8 %collective-permute-start.5 = (f32[8,1,2048]{2,1,0:T(1,128)S(1)}, f32[8,1,2048]{2,1,0:T(1,128)S(1)}, u32[]{:S(2)}, u32[]{:S(2)}) collective-permute-start(f32[8,1,2048]{2,1,0:T(1,128)S(1)} %get-tuple-element.11), channel_id=1, source_target_pairs={{0,1},{1,2},{2,3},{3,4},{4,5},{5,6},{6,7},{7,8},{8,9},{9,10},{10,1... | collective-permute-start | bytes 196616 | tf_op jit(solution)/shard_map/ppermute | solution.py:17
  119.2 22.1 %collective-permute-start.4 = (f32[8,1,2048]{2,1,0:T(1,128)S(1)}, f32[8,1,2048]{2,1,0:T(1,128)S(1)}, u32[]{:S(2)}, u32[]{:S(2)}) collective-permute-start(f32[8,1,2048]{2,1,0:T(1,128)S(1)} %get-tuple-element.12), channel_id=1, source_target_pairs={{1,0},{2,1},{3,2},{4,3},{5,4},{6,5},{7,6},{8,7},{9,8},{10,9},{11,1... | collective-permute-start | bytes 196616 | tf_op jit(solution)/shard_map/ppermute | solution.py:19
  121.4 0.8 copy-start.15
  151.0 1.9 %copy-start.8 = (f32[8,16,16,128]{3,2,1,0:T(8,128)S(1)}, f32[8,16,16,128]{3,2,1,0:T(8,128)}, u32[]{:S(2)}) copy-start(f32[8,16,16,128]{3,2,1,0:T(8,128)} %fusion.9) | copy-start | bytes 3145732
  152.7 1.2 copy-start.3
  152.7 1.5 copy-start.5
  156.1 2.4 %copy-start.12 = (f32[16,2048]{1,0:T(8,128)S(1)}, f32[16,2048]{1,0:T(8,128)}, u32[]{:S(2)}) copy-start(f32[16,2048]{1,0:T(8,128)} %param.17) | copy-start | bytes 393220
  156.2 2.4 %copy-start.20 = (f32[8]{0:T(128)S(1)}, f32[8]{0:T(128)}, u32[]{:S(2)}) copy-start(f32[8]{0:T(128)} %broadcast_multiply_fusion) | copy-start | bytes 100
where the time goes:
time: 163 us; the launch traced here: 162 us
  waiting for transfers between devices  43.3 us (27%)
  local copies, waits for them, and re-layouts  37 us (23%)
  starting transfers between devices  32.3 us (20%)
  matrix products  29.3 us (18%)
  other arithmetic  18.9 us (12%)
    ppermute x3, waiting for transfers between devices, padded_2(): lax.ppermute(tail, axis, [(i, (i + 1) % count) for i in range(ends)])  38.5 us
    all_to_all x3, starting transfers between devices, potential_grad(): lax.all_to_all(outgoing, 'row', split_axis=1, concat_axis=1, tiled=True)  15.8 us
    dot_general x3, matrix products, potential_grad(): jnp.einsum('crnk,qkl->qcrnl', blocks, kind_blocks, precision=highest)  13.5 us
    unnamed x51, local copies, waits for them, and re-layouts  10.4 us
    ppermute x3, starting transfers between devices, padded_2(): lax.ppermute(tail, axis, [(i, (i + 1) % count) for i in range(ends)])  10.1 us
    reshape x6, local copies, waits for them, and re-layouts, potential_grad(): flat_blocks = current.reshape(chains, strip_rows * per_row, block_width)  7.88 us
    ppermute x3, starting transfers between devices, padded_2(): lax.ppermute(head, axis, [((i + 1) % count, i) for i in range(ends)])  6.42 us
    dot_general x3, matrix products, potential_grad(): jnp.einsum('cbk,kl->cbl', lax.all_to_all(outgoing, 'row', split_axis=1, c...  6.11 us
  transfers between devices with their start and end apart: 9, of which 6 were waited for; matrix products, arithmetic and copies ran while one was open for 16% of the time, Pallas kernels for 0%

commit v1 on v0

v1 whole, which is shorter than its diff:
```python
import functools

import jax
import jax.numpy as jnp
from jax import lax
from jax.experimental import pallas as pl
from jax.experimental.pallas import tpu as pltpu
from jax.sharding import PartitionSpec as P

MESH = pl.DeviceIdType.MESH
bf16 = jnp.bfloat16
f32 = jnp.float32


def split(value):
    high = value.astype(bf16)
    low = (value - high.astype(f32)).astype(bf16)
    return high, low


def dot(a, b):
    return jnp.dot(a, b, preferred_element_type=f32)


def kernel(
    n,
    order_ref,
    pos_ref,
    x_ref,
    p_ref,
    step_ref,
    counts_ref,
    exposure_ref,
    diag_ref,
    kind_ref,
    kb_ref,
    vert_ref,
    match_ref,
    newx_ref,
    newp_ref,
    half_ref,
    w_ref,
    moved_ref,
    wfull_ref,
    w2_ref,
    q1_ref,
    q2_ref,
    vh_ref,
    vl_ref,
    kh_ref,
    kl_ref,
    uh_ref,
    ul_ref,
    mh_ref,
    ml_ref,
    send0,
    send1,
    send2,
    recv0,
    recv1,
    recv2,
    halo0,
    halo1,
    halo2,
    send_sem,
    recv_sem,
    edge_send,
    edge_recv,
):
    me = lax.axis_index("row")
    blocks, chains, width = x_ref.shape
    kinds = kb_ref.shape[0]
    per = 16
    rows = blocks // per
    lines = per * chains
    pairs = blocks // n
    sends = (send0, send1, send2)
    recvs = (recv0, recv1, recv2)
    halos = (halo0, halo1, halo2)

    barrier = pltpu.get_barrier_semaphore()

    @pl.loop(1, n)
    def _(d):
        pl.semaphore_signal(
            barrier, inc=1, device_id={"row": lax.rem(me + d, n)}, device_id_type=MESH
        )

    pl.semaphore_wait(barrier, n - 1)

    def edge_copy(src, phase, down):
        where = blocks - per if down else 0
        side = 0 if down else 1
        peer = lax.rem(me + (1 if down else n - 1), n)
        return pltpu.make_async_remote_copy(
            src_ref=src.at[pl.ds(where, per)],
            dst_ref=halos[phase].at[side],
            send_sem=edge_send.at[phase, side],
            recv_sem=edge_recv.at[phase, side],
            device_id={"row": peer},
            device_id_type=MESH,
        )

    def start_edges(src, phase):
        @pl.when(me < n - 1)
        def _():
            edge_copy(src, phase, True).start()

        @pl.when(me > 0)
        def _():
            edge_copy(src, phase, False).start()

    def wait_edges(src, phase):
        @pl.when(me > 0)
        def _():
            edge_copy(src, phase, True).wait_recv()

        @pl.when(me < n - 1)
        def _():
            edge_copy(src, phase, False).wait_recv()

    def drain_edges(src, phase):
        @pl.when(me < n - 1)
        def _():
            edge_copy(src, phase, True).wait_send()

        @pl.when(me > 0)
        def _():
            edge_copy(src, phase, False).wait_send()

    def slab_copy(phase, peer, here, there):
        return pltpu.make_async_remote_copy(
            src_ref=sends[phase].at[pl.ds(peer * pairs, pairs)],
            dst_ref=recvs[phase].at[pl.ds(here * pairs, pairs)],
            send_sem=send_sem.at[phase, peer],
            recv_sem=recv_sem.at[phase, there],
            device_id={"row": peer},
            device_id_type=MESH,
        )

    def start_exchange(src, phase):
        @pl.loop(0, n - 1)
        def _(k):
            peer = lax.rem(me + 1 + lax.rem(n // 2 - 1 + k, n - 1), n)
            for i in range(pairs):
                sends[phase][peer * pairs + i] = src[order_ref[peer * pairs + i]]
            slab_copy(phase, peer, me, me).start()

        for i in range(pairs):
            recvs[phase][me * pairs + i] = src[order_ref[me * pairs + i]]

    def wait_exchange(phase):
        @pl.loop(1, n)
        def _(d):
            peer = lax.rem(me + d, n)
            slab_copy(phase, peer, me, peer).wait_recv()

    def drain_exchange(phase):
        @pl.loop(1, n)
        def _(d):
            peer = lax.rem(me + d, n)
            slab_copy(phase, peer, me, me).wait_send()

    start_edges(x_ref, 0)
    start_exchange(x_ref, 0)

    for q in range(kinds):
        high, low = split(kb_ref[q])
        kh_ref[:width, q * width : (q + 1) * width] = high
        kh_ref[width:, q * width : (q + 1) * width] = high
        kl_ref[:, q * width : (q + 1) * width] = low
    high, low = split(vert_ref[...].T)
    uh_ref[:width] = high
    ul_ref[:width] = low
    high, low = split(vert_ref[...])
    uh_ref[width:] = high
    ul_ref[width:] = low
    high, low = split(match_ref[...])
    mh_ref[:width] = high
    mh_ref[width:] = high
    ml_ref[...] = low

    step = step_ref[...][None]
    tile = (per, chains, width)

    def times_match(value):
        high, low = split(value)
        both = jnp.concatenate([high, low], axis=1)
        return dot(both, mh_ref[...]) + dot(high, ml_ref[...])

    def fill(src):
        @pl.loop(0, rows)
        def _(r):
            high, low = split(src[pl.ds(r * per, per)].reshape(lines, width))
            vh_ref[pl.ds((r + 1) * lines, lines)] = high
            vl_ref[pl.ds((r + 1) * lines, lines)] = low

    def fill_halo(phase):
        for side, outside in ((0, me == 0), (1, me == n - 1)):
            value = halos[phase][side].reshape(lines, width)
            value = jnp.where(outside, jnp.zeros_like(value), value)
            high, low = split(value)
            at = side * (rows + 1) * lines
            vh_ref[at : at + lines] = high
            vl_ref[at : at + lines] = low

    def local_grad(src, r):
        here = pl.ds(r * per, per)
        vh = vh_ref[pl.ds((r + 1) * lines, lines)]
        vl = vl_ref[pl.ds((r + 1) * lines, lines)]
        within = dot(jnp.concatenate([vh, vl], axis=1), kh_ref[...]) + dot(vh, kl_ref[...])
        kind = jnp.broadcast_to(kind_ref[here], tile)
        own = within[:, :width].reshape(tile)
        for q in range(1, kinds):
            own = jnp.where(kind == q, within[:, q * width : (q + 1) * width].reshape(tile), own)
        above, below = pl.ds(r * lines, lines), pl.ds((r + 2) * lines, lines)
        sh = jnp.concatenate([vh_ref[below], vh_ref[above]], axis=1)
        sl = jnp.concatenate([vl_ref[below], vl_ref[above]], axis=1)
        vertical = dot(sh, uh_ref[...]) + dot(sl, uh_ref[...]) + dot(sh, ul_ref[...])
        value = src[here]
        return (
            own
            - vertical.reshape(tile)
            + diag_ref[here] * value
            - counts_ref[here]
            + exposure_ref[here] * jnp.exp(value)
        )

    def all_rows(src, phase, use):
        fill(src)

        @pl.loop(1, rows - 1)
        def _(r):
            use(r, local_grad(src, r))

        wait_edges(src, phase)
        fill_halo(phase)

        @pl.loop(0, 2)
        def _(e):
            r = e * (rows - 1)
            use(r, local_grad(src, r))

    def received(phase, r):
        return jnp.concatenate(
            [recvs[phase][pos_ref[r * per + i]] for i in range(per)], axis=0
        )

    def use_first(r, grad):
        here = pl.ds(r * per, per)
        half = p_ref[here] - 0.5 * step * grad
        half_ref[here] = half
        w_ref[here] = x_ref[here] + step * half

    all_rows(x_ref, 0, use_first)
    start_exchange(w_ref, 1)

    @pl.loop(0, rows)
    def _(r):
        here = pl.ds(r * per, per)
        product = times_match(x_ref[here].reshape(lines, width)).reshape(tile)
        q1_ref[here] = 0.5 * step * step * product

    wait_exchange(0)

    @pl.loop(0, rows)
    def _(r):
        here = pl.ds(r * per, per)
        matched = times_match(received(0, r)).reshape(tile)
        half_ref[here] = half_ref[here] + 0.5 * step * matched
        moved_ref[here] = w_ref[here] + 0.5 * step * step * matched

    start_edges(moved_ref, 1)

    def use_second(r, grad):
        here = pl.ds(r * per, per)
        full = half_ref[here] - step * grad
        wfull_ref[here] = full
        w2_ref[here] = moved_ref[here] + step * full

    all_rows(moved_ref, 1, use_second)
    start_exchange(w2_ref, 2)

    @pl.loop(0, rows)
    def _(r):
        here = pl.ds(r * per, per)
        product = times_match(moved_ref[here].reshape(lines, width)).reshape(tile)
        q2_ref[here] = step * step * product

    wait_exchange(1)

    @pl.loop(0, rows)
    def _(r):
        here = pl.ds(r * per, per)
        value = received(1, r) + q1_ref[here].reshape(lines, width)
        matched = times_match(value).reshape(tile)
        wfull_ref[here] = wfull_ref[here] + step * matched
        newx_ref[here] = w2_ref[here] + step * step * matched

    start_edges(newx_ref, 2)

    def use_third(r, grad):
        here = pl.ds(r * per, per)
        newp_ref[here] = wfull_ref[here] - 0.5 * step * grad

    all_rows(newx_ref, 2, use_third)
    wait_exchange(2)

    @pl.loop(0, rows)
    def _(r):
        here = pl.ds(r * per, per)
        value = received(2, r) + q2_ref[here].reshape(lines, width)
        matched = times_match(value).reshape(tile)
        newp_ref[here] = newp_ref[here] + 0.5 * step * matched

    for phase, src in enumerate((x_ref, moved_ref, newx_ref)):
        drain_edges(src, phase)
        drain_exchange(phase)


def body(
    positions,
    momenta,
    step_size,
    counts,
    exposure,
    precision_diag,
    kind_blocks,
    vertical_coupling,
    matched_coupling,
    partner,
    block_kind,
):
    n = lax.axis_size("row")
    chains, rows, cols = positions.shape
    kinds, width = kind_blocks.shape[:2]
    per = cols // width
    blocks = rows * per

    ids = jnp.arange(blocks, dtype=jnp.int32)
    key = (partner // blocks) * blocks + ids
    slot = jnp.sum((key[None, :] < key[:, None]).astype(jnp.int32), axis=1)
    pos = jnp.sum((partner[None, :] < partner[:, None]).astype(jnp.int32), axis=1)
    order = jnp.sum(jnp.where(slot[None, :] == ids[:, None], ids[None, :], 0), axis=1)

    def to_blocks(v):
        return v.reshape(chains, rows, per, width).transpose(1, 2, 0, 3).reshape(
            blocks, chains, width
        )

    def from_blocks(v):
        return v.reshape(rows, per, chains, width).transpose(2, 0, 1, 3).reshape(
            chains, rows, cols
        )

    def unit(v):
        return v.reshape(blocks, 1, width)

    kind = jnp.broadcast_to(block_kind.reshape(blocks, 1, 1), (blocks, 1, width))
    step = jnp.broadcast_to(step_size[:, None], (chains, width))
    vmem = pl.BlockSpec(memory_space=pltpu.VMEM)
    smem = pl.BlockSpec(memory_space=pltpu.SMEM)
    field = (blocks, chains, width)
    lines = per * chains
    big = lambda: pltpu.VMEM(field, f32)
    newx, newp = pl.pallas_call(
        functools.partial(kernel, n),
        out_shape=(jax.ShapeDtypeStruct(field, f32), jax.ShapeDtypeStruct(field, f32)),
        in_specs=[smem] * 2 + [vmem] * 10,
        out_specs=(vmem, vmem),
        scratch_shapes=[big() for _ in range(7)]
        + [
            pltpu.VMEM(((rows + 2) * lines, width), bf16),
            pltpu.VMEM(((rows + 2) * lines, width), bf16),
            pltpu.VMEM((2 * width, kinds * width), bf16),
            pltpu.VMEM((width, kinds * width), bf16),
            pltpu.VMEM((2 * width, width), bf16),
            pltpu.VMEM((2 * width, width), bf16),
            pltpu.VMEM((2 * width, width), bf16),
            pltpu.VMEM((width, width), bf16),
        ]
        + [big() for _ in range(6)]
        + [pltpu.VMEM((2, per, chains, width), f32) for _ in range(3)]
        + [
            pltpu.SemaphoreType.DMA((3, n)),
            pltpu.SemaphoreType.DMA((3, n)),
            pltpu.SemaphoreType.DMA((3, 2)),
            pltpu.SemaphoreType.DMA((3, 2)),
        ],
        compiler_params=pltpu.CompilerParams(
            collective_id=0, has_side_effects=True, vmem_limit_bytes=48 * 1024 * 1024
        ),
    )(
        order,
        pos,
        to_blocks(positions),
        to_blocks(momenta),
        step,
        unit(counts),
        unit(exposure),
        unit(precision_diag),
        kind,
        kind_blocks,
        vertical_coupling,
        matched_coupling,
    )
    return from_blocks(newx), from_blocks(newp)


def solution(mesh):
    return jax.shard_map(
        body,
        mesh=mesh,
        in_specs=(
            P(None, ("groups", "row"), None),
            P(None, ("groups", "row"), None),
            P("groups"),
            P(("groups", "row"), None),
            P(("groups", "row"), None),
            P(("groups", "row"), None),
            P(),
            P(),
            P(),
            P(("groups", "row")),
            P(("groups", "row"), None),
        ),
        out_specs=(P(None, ("groups", "row"), None), P(None, ("groups", "row"), None)),
        check_vma=False,
    )
```

time: 163 us -> 94.6 us (0.58)
  Pallas kernels: 0 us -> 81.4 us
  waiting for transfers between devices: 43.3 us -> 0 us
  starting transfers between devices: 32.3 us -> 0 us
  matrix products: 29.3 us -> 0 us
  local copies, waits for them, and re-layouts: 37 us -> 10.2 us
  other arithmetic: 18.9 us -> 1.86 us
    pallas_call x0 -> x1, Pallas kernels: none -> 81.4 us  [body(): pl.pallas_call(functools.partial(kernel, n), out_shape=(jax.ShapeDtypeStr...]
    ppermute x6 -> x0, waiting for transfers between devices: 43.3 us -> none  [the longest x3 38.5 us: padded_2(): lax.ppermute(tail, axis, [(i, (i + 1) % count) for i in range(ends)])]
    dot_general x12 -> x0, matrix products: 29.3 us -> none  [the longest x3 13.5 us: potential_grad(): jnp.einsum('crnk,qkl->qcrnl', blocks, kind_blocks, precision=highest)]
    ppermute x6 -> x0, starting transfers between devices: 16.5 us -> none  [the longest x3 10.1 us: padded_2(): lax.ppermute(tail, axis, [(i, (i + 1) % count) for i in range(ends)])]
    all_to_all x3 -> x0, starting transfers between devices: 15.8 us -> none  [potential_grad(): lax.all_to_all(outgoing, 'row', split_axis=1, concat_axis=1, tiled=True)]
    gather x6 -> x0, local copies, waits for them, and re-layouts: 12 us -> none  [the longest x3 5.99 us: potential_grad(): outgoing = jnp.take(flat_blocks, send_order, axis=1)]
    select_n x9 -> x0, other arithmetic: 8.91 us -> none  [the longest x4 5.85 us: potential_grad(): outgoing = jnp.take(flat_blocks, send_order, axis=1)]
    reshape x9 -> x7, local copies, waits for them, and re-layouts: 11.6 us -> 3.96 us  [the longest x2 2.26 us: from_blocks(): v.reshape(rows, per, chains, width).transpose(2, 0, 1, 3)]
  transfers between devices with their start and end apart: 9 -> 0, of which waited for: 6 -> 0; matrix products, arithmetic and copies ran while one was open for 16% -> 0% of each run, Pallas kernels for 0% -> 0%
where the time goes in v1:
time: 94.6 us; the launch traced here: 94.3 us
  Pallas kernels  81.4 us (86%)
  local copies, waits for them, and re-layouts  10.2 us (11%)
  other arithmetic  1.86 us (2%)
    pallas_call x1, Pallas kernels, body(): pl.pallas_call(functools.partial(kernel, n), out_shape=(jax.ShapeDtypeStr...  81.4 us
    unnamed x16, local copies, waits for them, and re-layouts  4 us
    reshape x2, local copies, waits for them, and re-layouts, from_blocks(): v.reshape(rows, per, chains, width).transpose(2, 0, 1, 3)  2.26 us

profile of v1, /device:TPU:15, one launch (start us, length us, event | category | flops | bytes accessed | tf_op | source)
XLA Modules:
  0.0 94.3 jit_solution(13534501131594121228)
XLA Ops:
  0.6 0.0 copy-start.4
  0.6 0.8 broadcast_in_dim.21
  1.5 0.7 iota_add_fusion
  2.1 0.2 convert_reduce_fusion.1
  2.3 1.0 %convert_reduce_fusion = (s32[256]{0:T(256)S(1)}, s32[256]{0:T(256)S(1)}) fusion(s32[256]{0:T(256)} %param.20, s32[256]{0:T(256)S(1)} %convert_reduce_fusion.1), kind=kLoop, calls=%fused_computation | loop fusion | flops 392704 | bytes 4096 | tf_op jit(solution)/shard_map/reduce_sum | solution.py:343
  3.3 0.7 broadcast_in_dim.20.step_ref
  4.0 0.3 broadcast_in_dim.36.kind_ref
  4.4 0.0 copy-done.4
  4.4 0.0 copy-start.5
  4.4 0.2 reshape.51.counts_ref
  4.6 0.7 copy-done.5
  5.3 0.0 copy-start.6
  5.3 0.2 reshape.52.exposure_ref
  5.5 0.7 copy-done.6
  6.2 0.2 reshape.53.diag_ref
  6.4 1.4 %copy.21 = f32[16,8,16,128]{3,2,1,0:T(8,128)S(1)} copy(f32[16,8,16,128]{3,1,2,0:T(8,128)} %bitcast.30) | data formatting | bytes 2097152
  7.8 0.0 copy-start.3
  7.8 0.6 copy.17
  8.4 0.6 copy-done.3
  9.0 0.2 copy.22
  9.2 0.0 copy-start
  9.2 0.0 copy-start.1
  9.2 0.0 copy-start.2
  9.2 0.6 copy.18
  9.8 0.3 copy-done
  10.1 0.0 copy-done.1
  10.1 0.0 copy-done.2
  10.1 81.4 %shard_map.122 = (f32[256,8,128]{2,1,0:T(8,128)S(1)}, f32[256,8,128]{2,1,0:T(8,128)S(1)}) custom-call(s32[256]{0:T(256)S(1)} %get-tuple-element.7.order_ref, s32[256]{0:T(256)S(1)} %get-tuple-element.6.pos_ref, f32[256,8,128]{2,1,0:T(8,128)S(1)} %bitcast.24, f32[256,8,128]{2,1,0:T(8,128)S(1)} %bitcast.25, f32[8,128]{1,0:T(8,128)S(1)} %broadcast_in_dim.20.step_ref, ...), custom_call_target="tpu_custom_call" | custom-call | tf_op jit(solution)/shard_map/pallas_call | solution.py:366
  91.6 0.2 copy.19
  91.8 1.1 %reshape.55 = f32[8,16,2048]{2,1,0:T(8,128)} reshape(f32[8,16,16,128]{3,2,1,0:T(8,128)S(1)} %copy.19) | data formatting | bytes 2097152 | tf_op jit(solution)/shard_map/reshape | solution.py:352
  92.9 0.2 copy.20
  93.1 1.1 %reshape.57 = f32[8,16,2048]{2,1,0:T(8,128)} reshape(f32[8,16,16,128]{3,2,1,0:T(8,128)S(1)} %copy.20) | data formatting | bytes 2097152 | tf_op jit(solution)/shard_map/reshape | solution.py:352
Async XLA Ops:
  0.6 3.7 %copy-start.4 = (f32[16,2048]{1,0:T(8,128)S(1)}, f32[16,2048]{1,0:T(8,128)}, u32[]{:S(2)}) copy-start(f32[16,2048]{1,0:T(8,128)} %param.14) | copy-start | bytes 393220
  4.4 0.9 copy-start.5
  5.3 0.9 copy-start.6
  7.8 1.2 %copy-start.3 = (f32[8,16,2048]{2,1,0:T(8,128)S(1)}, f32[8,16,2048]{2,1,0:T(8,128)}, u32[]{:S(2)}) copy-start(f32[8,16,2048]{2,1,0:T(8,128)} %param.12) | copy-start | bytes 3145732
  9.2 1.0 %copy-start = (f32[4,128,128]{2,1,0:T(8,128)S(1)}, f32[4,128,128]{2,1,0:T(8,128)}, u32[]{:S(2)}) copy-start(f32[4,128,128]{2,1,0:T(8,128)} %kb_ref.1) | copy-start | bytes 786436
  9.2 0.9 %copy-start.1 = (f32[128,128]{1,0:T(8,128)S(1)}, f32[128,128]{1,0:T(8,128)}, u32[]{:S(2)}) copy-start(f32[128,128]{1,0:T(8,128)} %vert_ref.1) | copy-start | bytes 196612
  9.2 0.9 copy-start.2

commit v2 on v1

--- a/solution.py
+++ b/solution.py
@@ -26,16 +26,19 @@
     n,
     order_ref,
     pos_ref,
+    step_ref,
+    kind_ref,
+    xin_ref,
+    pin_ref,
+    counts_in,
+    exposure_in,
+    diag_in,
+    kb_in,
+    vert_in,
+    match_in,
+    xout_ref,
+    pout_ref,
     x_ref,
-    p_ref,
-    step_ref,
-    counts_ref,
-    exposure_ref,
-    diag_ref,
-    kind_ref,
-    kb_ref,
-    vert_ref,
-    match_ref,
     newx_ref,
     newp_ref,
     half_ref,
@@ -66,12 +69,23 @@
     recv_sem,
     edge_send,
     edge_recv,
+    xheld,
+    pheld,
+    xoheld,
+    poheld,
+    local_sem,
+    counts_ref,
+    exposure_ref,
+    diag_ref,
+    kb_ref,
+    vert_ref,
+    match_ref,
+    small_sem,
 ):
     me = lax.axis_index("row")
     blocks, chains, width = x_ref.shape
     kinds = kb_ref.shape[0]
-    per = 16
-    rows = blocks // per
+    rows, per = kind_ref.shape
     lines = per * chains
     pairs = blocks // n
     sends = (send0, send1, send2)
@@ -80,12 +94,65 @@
 
     barrier = pltpu.get_barrier_semaphore()
 
+    @pl.loop(0, per)
+    def _(j):
+        pltpu.make_async_copy(
+            xin_ref.at[:, pl.ds(pl.multiple_of(j * width, width), width)],
+            xheld.at[j],
+            local_sem.at[0, j],
+        ).start()
+
     @pl.loop(1, n)
     def _(d):
         pl.semaphore_signal(
             barrier, inc=1, device_id={"row": lax.rem(me + d, n)}, device_id_type=MESH
         )
 
+    def panel(whole, held, which, j, out=False):
+        far, near = whole.at[:, pl.ds(pl.multiple_of(j * width, width), width)], held.at[j]
+        if out:
+            far, near = near, far
+        return pltpu.make_async_copy(far, near, local_sem.at[which, j])
+
+    def take_row(held, r):
+        return jnp.stack([held[j, pl.ds(r, chains, stride=rows), :] for j in range(per)])
+
+    def put_row(held, r, value):
+        for j in range(per):
+            held[j, pl.ds(r, chains, stride=rows), :] = value[j]
+
+    def start_panels(whole, held, which, out=False):
+        @pl.loop(0, per)
+        def _(j):
+            panel(whole, held, which, j, out).start()
+
+    def wait_panels(whole, held, which, out=False):
+        @pl.loop(0, per)
+        def _(j):
+            panel(whole, held, which, j, out).wait()
+
+    @pl.loop(0, per)
+    def _(j):
+        panel(xin_ref, xheld, 0, j).wait()
+        for r in range(rows):
+            x_ref[r * per + j] = xheld[j, pl.ds(r, chains, stride=rows), :]
+
+    small = [
+        pltpu.make_async_copy(far, near, small_sem.at[i])
+        for i, (far, near) in enumerate(
+            (
+                (kb_in, kb_ref),
+                (vert_in, vert_ref),
+                (match_in, match_ref),
+                (counts_in, counts_ref),
+                (exposure_in, exposure_ref),
+                (diag_in, diag_ref),
+            )
+        )
+    ]
+    for copy in small:
+        copy.start()
+    start_panels(pin_ref, pheld, 1)
     pl.semaphore_wait(barrier, n - 1)
 
     def edge_copy(src, phase, down):
@@ -164,6 +231,8 @@
     start_edges(x_ref, 0)
     start_exchange(x_ref, 0)
 
+    for copy in small:
+        copy.wait()
     for q in range(kinds):
         high, low = split(kb_ref[q])
         kh_ref[:width, q * width : (q + 1) * width] = high
@@ -180,8 +249,21 @@
     mh_ref[width:] = high
     ml_ref[...] = low
 
-    step = step_ref[...][None]
     tile = (per, chains, width)
+    chain = lax.broadcasted_iota(jnp.int32, (chains, width), 0)
+    step = jnp.zeros((chains, width), f32)
+    for c in range(chains):
+        step = jnp.where(chain == c, step_ref[c], step)
+    step = step[None]
+
+    def unit_row(src, r):
+        line = src[pl.ds(r, 1), :]
+        return jnp.stack(
+            [
+                jnp.broadcast_to(line[:, j * width : (j + 1) * width], (chains, width))
+                for j in range(per)
+            ]
+        )
 
     def times_match(value):
         high, low = split(value)
@@ -209,7 +291,7 @@
         vh = vh_ref[pl.ds((r + 1) * lines, lines)]
         vl = vl_ref[pl.ds((r + 1) * lines, lines)]
         within = dot(jnp.concatenate([vh, vl], axis=1), kh_ref[...]) + dot(vh, kl_ref[...])
-        kind = jnp.broadcast_to(kind_ref[here], tile)
+        kind = jnp.stack([jnp.full((chains, width), kind_ref[r, j]) for j in range(per)])
         own = within[:, :width].reshape(tile)
         for q in range(1, kinds):
             own = jnp.where(kind == q, within[:, q * width : (q + 1) * width].reshape(tile), own)
@@ -221,9 +303,9 @@
         return (
             own
             - vertical.reshape(tile)
-            + diag_ref[here] * value
-            - counts_ref[here]
-            + exposure_ref[here] * jnp.exp(value)
+            + unit_row(diag_ref, r) * value
+            - unit_row(counts_ref, r)
+            + unit_row(exposure_ref, r) * jnp.exp(value)
         )
 
     def all_rows(src, phase, use):
@@ -248,10 +330,11 @@
 
     def use_first(r, grad):
         here = pl.ds(r * per, per)
-        half = p_ref[here] - 0.5 * step * grad
+        half = take_row(pheld, r) - 0.5 * step * grad
         half_ref[here] = half
         w_ref[here] = x_ref[here] + step * half
 
+    wait_panels(pin_ref, pheld, 1)
     all_rows(x_ref, 0, use_first)
     start_exchange(w_ref, 1)
 
@@ -295,9 +378,12 @@
         value = received(1, r) + q1_ref[here].reshape(lines, width)
         matched = times_match(value).reshape(tile)
         wfull_ref[here] = wfull_ref[here] + step * matched
-        newx_ref[here] = w2_ref[here] + step * step * matched
+        newx = w2_ref[here] + step * step * matched
+        newx_ref[here] = newx
+        put_row(xoheld, r, newx)
 
     start_edges(newx_ref, 2)
+    start_panels(xout_ref, xoheld, 2, True)
 
     def use_third(r, grad):
         here = pl.ds(r * per, per)
@@ -311,11 +397,14 @@
         here = pl.ds(r * per, per)
         value = received(2, r) + q2_ref[here].reshape(lines, width)
         matched = times_match(value).reshape(tile)
-        newp_ref[here] = newp_ref[here] + 0.5 * step * matched
-
+        put_row(poheld, r, newp_ref[here] + 0.5 * step * matched)
+
+    start_panels(pout_ref, poheld, 3, True)
     for phase, src in enumerate((x_ref, moved_ref, newx_ref)):
         drain_edges(src, phase)
         drain_exchange(phase)
+    wait_panels(xout_ref, xoheld, 2, True)
+    wait_panels(pout_ref, poheld, 3, True)
 
 
 def body(
@@ -343,32 +432,18 @@
     pos = jnp.sum((partner[None, :] < partner[:, None]).astype(jnp.int32), axis=1)
     order = jnp.sum(jnp.where(slot[None, :] == ids[:, None], ids[None, :], 0), axis=1)
 
-    def to_blocks(v):
-        return v.reshape(chains, rows, per, width).transpose(1, 2, 0, 3).reshape(
-            blocks, chains, width
-        )
-
-    def from_blocks(v):
-        return v.reshape(rows, per, chains, width).transpose(2, 0, 1, 3).reshape(
-            chains, rows, cols
-        )
-
-    def unit(v):
-        return v.reshape(blocks, 1, width)
-
-    kind = jnp.broadcast_to(block_kind.reshape(blocks, 1, 1), (blocks, 1, width))
-    step = jnp.broadcast_to(step_size[:, None], (chains, width))
-    vmem = pl.BlockSpec(memory_space=pltpu.VMEM)
+    hbm = pl.BlockSpec(memory_space=pl.ANY)
     smem = pl.BlockSpec(memory_space=pltpu.SMEM)
     field = (blocks, chains, width)
     lines = per * chains
     big = lambda: pltpu.VMEM(field, f32)
+    flat = (chains * rows, cols)
     newx, newp = pl.pallas_call(
         functools.partial(kernel, n),
-        out_shape=(jax.ShapeDtypeStruct(field, f32), jax.ShapeDtypeStruct(field, f32)),
-        in_specs=[smem] * 2 + [vmem] * 10,
-        out_specs=(vmem, vmem),
-        scratch_shapes=[big() for _ in range(7)]
+        out_shape=(jax.ShapeDtypeStruct(flat, f32), jax.ShapeDtypeStruct(flat, f32)),
+        in_specs=[smem] * 4 + [hbm] * 8,
+        out_specs=(hbm, hbm),
+        scratch_shapes=[big() for _ in range(10)]
         + [
             pltpu.VMEM(((rows + 2) * lines, width), bf16),
             pltpu.VMEM(((rows + 2) * lines, width), bf16),
@@ -386,25 +461,34 @@
             pltpu.SemaphoreType.DMA((3, n)),
             pltpu.SemaphoreType.DMA((3, 2)),
             pltpu.SemaphoreType.DMA((3, 2)),
+        ]
+        + [pltpu.VMEM((per, chains * rows, width), f32) for _ in range(4)]
+        + [pltpu.SemaphoreType.DMA((4, per))]
+        + [pltpu.VMEM((rows, cols), f32) for _ in range(3)]
+        + [
+            pltpu.VMEM((kinds, width, width), f32),
+            pltpu.VMEM((width, width), f32),
+            pltpu.VMEM((width, width), f32),
+            pltpu.SemaphoreType.DMA((6,)),
         ],
         compiler_params=pltpu.CompilerParams(
-            collective_id=0, has_side_effects=True, vmem_limit_bytes=48 * 1024 * 1024
+            collective_id=0, has_side_effects=True, vmem_limit_bytes=60 * 1024 * 1024
         ),
     )(
         order,
         pos,
-        to_blocks(positions),
-        to_blocks(momenta),
-        step,
-        unit(counts),
-        unit(exposure),
-        unit(precision_diag),
-        kind,
+        step_size,
+        block_kind,
+        positions.reshape(flat),
+        momenta.reshape(flat),
+        counts,
+        exposure,
+        precision_diag,
         kind_blocks,
         vertical_coupling,
         matched_coupling,
     )
-    return from_blocks(newx), from_blocks(newp)
+    return newx.reshape(positions.shape), newp.reshape(positions.shape)
 
 
 def solution(mesh):

time: 94.6 us -> 89.4 us (0.945)
  local copies, waits for them, and re-layouts: 10.2 us -> 4.03 us
  Pallas kernels: 81.4 us -> 83.4 us
    reshape x7 -> x0, local copies, waits for them, and re-layouts: 3.96 us -> none  [the longest x2 2.26 us: from_blocks(): v.reshape(rows, per, chains, width).transpose(2, 0, 1, 3)]
    pallas_call x1, Pallas kernels: 81.4 us -> 83.4 us  [body(): pl.pallas_call(functools.partial(kernel, n), out_shape=(jax.ShapeDtypeStr...]
    broadcast_in_dim x3 -> x0, local copies, waits for them, and re-layouts: 1.87 us -> none  [the longest x2 1.13 us: body(): jnp.broadcast_to(block_kind.reshape(blocks, 1, 1), (blocks, 1, width))]
    unnamed x16 -> x6, local copies, waits for them, and re-layouts: 4 us -> 4.03 us
where the time goes in v2:
time: 89.4 us; the launch traced here: 89.1 us
  Pallas kernels  83.4 us (93%)
  local copies, waits for them, and re-layouts  4.03 us (5%)
  other arithmetic  0.99 us (1%)
    pallas_call x1, Pallas kernels, body(): pl.pallas_call(functools.partial(kernel, n), out_shape=(jax.ShapeDtypeStr...  83.4 us
    unnamed x6, local copies, waits for them, and re-layouts  4.03 us

profile of v2, /device:TPU:15, one launch (start us, length us, event | category | flops | bytes accessed | tf_op | source)
XLA Modules:
  0.0 89.1 jit_solution(3297264944160371592)
XLA Ops:
  0.6 0.0 copy-start.1
  0.6 0.7 copy-done.1
  1.3 0.2 convert_reduce_fusion.1
  1.5 0.8 convert_reduce_fusion
  2.3 83.4 %shard_map.122 = (f32[128,2048]{1,0:T(8,128)}, f32[128,2048]{1,0:T(8,128)}) custom-call(s32[256]{0:T(256)} %get-tuple-element.7.order_ref, s32[256]{0:T(256)} %get-tuple-element.6.pos_ref, f32[8]{0:T(128)} %step_ref.1, s32[16,16]{1,0:T(8,128)} %kind_ref.1, f32[128,2048]{1,0:T(8,128)} %bitcast.6, f32[128,2048]{1,0:T(8,128)} %bitcast.7, f32[16,2048]{1,0:T(8,128)} %counts_in.1, ...), custom_call_target="tpu_custom_call" | custom-call | tf_op jit(solution)/shard_map/pallas_call | solution.py:441
  85.7 0.0 copy-start
  85.8 2.4 %copy.15 = f32[8,16,2048]{2,1,0:T(8,128)} copy(f32[8,16,2048]{2,1,0:T(8,128)} %bitcast.5) | data formatting | bytes 2097152
  88.1 0.0 copy-done
  88.1 1.0 %copy.16 = f32[8,16,2048]{2,1,0:T(8,128)} copy(f32[8,16,2048]{2,1,0:T(8,128)S(1)} %bitcast.4) | data formatting | bytes 2097152
  (1 shorter events, 0.0 us)
Async XLA Ops:
  0.6 0.7 copy-start.1
  85.7 2.4 %copy-start = (f32[128,2048]{1,0:T(8,128)S(1)}, f32[128,2048]{1,0:T(8,128)}, u32[]{:S(2)}) copy-start(f32[128,2048]{1,0:T(8,128)} %get-tuple-element.5) | copy-start | bytes 3145732

commit v3 on v2

--- a/solution.py
+++ b/solution.py
@@ -205,16 +205,19 @@
             device_id_type=MESH,
         )
 
-    def start_exchange(src, phase):
-        @pl.loop(0, n - 1)
+    early = n // 2
+
+    def start_exchange(src, phase, first, last):
+        @pl.loop(first, last)
         def _(k):
-            peer = lax.rem(me + 1 + lax.rem(n // 2 - 1 + k, n - 1), n)
+            peer = lax.rem(me + 1 + k, n)
             for i in range(pairs):
                 sends[phase][peer * pairs + i] = src[order_ref[peer * pairs + i]]
             slab_copy(phase, peer, me, me).start()
 
-        for i in range(pairs):
-            recvs[phase][me * pairs + i] = src[order_ref[me * pairs + i]]
+        if first == 0:
+            for i in range(pairs):
+                recvs[phase][me * pairs + i] = src[order_ref[me * pairs + i]]
 
     def wait_exchange(phase):
         @pl.loop(1, n)
@@ -229,7 +232,7 @@
             slab_copy(phase, peer, me, me).wait_send()
 
     start_edges(x_ref, 0)
-    start_exchange(x_ref, 0)
+    start_exchange(x_ref, 0, 0, n - 1)
 
     for copy in small:
         copy.wait()
@@ -336,7 +339,7 @@
 
     wait_panels(pin_ref, pheld, 1)
     all_rows(x_ref, 0, use_first)
-    start_exchange(w_ref, 1)
+    start_exchange(w_ref, 1, 0, early)
 
     @pl.loop(0, rows)
     def _(r):
@@ -354,6 +357,7 @@
         moved_ref[here] = w_ref[here] + 0.5 * step * step * matched
 
     start_edges(moved_ref, 1)
+    start_exchange(w_ref, 1, early, n - 1)
 
     def use_second(r, grad):
         here = pl.ds(r * per, per)
@@ -362,7 +366,7 @@
         w2_ref[here] = moved_ref[here] + step * full
 
     all_rows(moved_ref, 1, use_second)
-    start_exchange(w2_ref, 2)
+    start_exchange(w2_ref, 2, 0, early)
 
     @pl.loop(0, rows)
     def _(r):
@@ -383,6 +387,7 @@
         put_row(xoheld, r, newx)
 
     start_edges(newx_ref, 2)
+    start_exchange(w2_ref, 2, early, n - 1)
     start_panels(xout_ref, xoheld, 2, True)
 
     def use_third(r, grad):

time: 89.4 us -> 88.5 us (0.990); the launches traced: 89.1 us -> 87.3 us
  Pallas kernels: 83.4 us -> 81.6 us
    pallas_call x1, Pallas kernels: 83.4 us -> 81.6 us  [body(): pl.pallas_call(functools.partial(kernel, n), out_shape=(jax.ShapeDtypeStr...]
where the time goes in v3:
time: 88.5 us; the launch traced here: 87.3 us
  Pallas kernels  81.6 us (92%)
  local copies, waits for them, and re-layouts  4.03 us (5%)
  other arithmetic  0.99 us (1%)
    pallas_call x1, Pallas kernels, body(): pl.pallas_call(functools.partial(kernel, n), out_shape=(jax.ShapeDtypeStr...  81.6 us
    unnamed x6, local copies, waits for them, and re-layouts  4.03 us

profile of v3, /device:TPU:15, one launch (start us, length us, event | category | flops | bytes accessed | tf_op | source)
XLA Modules:
  0.0 87.3 jit_solution(17218934948628371597)
XLA Ops:
  0.6 0.0 copy-start.1
  0.6 0.7 copy-done.1
  1.3 0.2 convert_reduce_fusion.1
  1.5 0.8 convert_reduce_fusion
  2.3 81.6 %shard_map.122 = (f32[128,2048]{1,0:T(8,128)}, f32[128,2048]{1,0:T(8,128)}) custom-call(s32[256]{0:T(256)} %get-tuple-element.7.order_ref, s32[256]{0:T(256)} %get-tuple-element.6.pos_ref, f32[8]{0:T(128)} %step_ref.1, s32[16,16]{1,0:T(8,128)} %kind_ref.1, f32[128,2048]{1,0:T(8,128)} %bitcast.6, f32[128,2048]{1,0:T(8,128)} %bitcast.7, f32[16,2048]{1,0:T(8,128)} %counts_in.1, ...), custom_call_target="tpu_custom_call" | custom-call | tf_op jit(solution)/shard_map/pallas_call | solution.py:446
  83.9 0.0 copy-start
  83.9 2.4 %copy.15 = f32[8,16,2048]{2,1,0:T(8,128)} copy(f32[8,16,2048]{2,1,0:T(8,128)} %bitcast.5) | data formatting | bytes 2097152
  86.3 0.0 copy-done
  86.3 1.0 %copy.16 = f32[8,16,2048]{2,1,0:T(8,128)} copy(f32[8,16,2048]{2,1,0:T(8,128)S(1)} %bitcast.4) | data formatting | bytes 2097152
  (1 shorter events, 0.0 us)
Async XLA Ops:
  0.6 0.7 copy-start.1
  83.9 2.4 %copy-start = (f32[128,2048]{1,0:T(8,128)S(1)}, f32[128,2048]{1,0:T(8,128)}, u32[]{:S(2)}) copy-start(f32[128,2048]{1,0:T(8,128)} %get-tuple-element.5) | copy-start | bytes 3145732

commit v4 on v3

--- a/solution.py
+++ b/solution.py
@@ -363,16 +363,19 @@
         here = pl.ds(r * per, per)
         full = half_ref[here] - step * grad
         wfull_ref[here] = full
-        w2_ref[here] = moved_ref[here] + step * full
+        ahead = moved_ref[here] + step * full
+        w2_ref[here] = ahead
+        half_ref[here] = times_match(ahead.reshape(lines, width)).reshape(tile)
 
     all_rows(moved_ref, 1, use_second)
-    start_exchange(w2_ref, 2, 0, early)
+    start_exchange(half_ref, 2, 0, early)
 
     @pl.loop(0, rows)
     def _(r):
         here = pl.ds(r * per, per)
         product = times_match(moved_ref[here].reshape(lines, width)).reshape(tile)
-        q2_ref[here] = step * step * product
+        twice = times_match((step * step * product).reshape(lines, width)).reshape(tile)
+        q2_ref[here] = 0.5 * step * twice
 
     wait_exchange(1)
 
@@ -387,12 +390,12 @@
         put_row(xoheld, r, newx)
 
     start_edges(newx_ref, 2)
-    start_exchange(w2_ref, 2, early, n - 1)
+    start_exchange(half_ref, 2, early, n - 1)
     start_panels(xout_ref, xoheld, 2, True)
 
     def use_third(r, grad):
         here = pl.ds(r * per, per)
-        newp_ref[here] = wfull_ref[here] - 0.5 * step * grad
+        newp_ref[here] = wfull_ref[here] + q2_ref[here] - 0.5 * step * grad
 
     all_rows(newx_ref, 2, use_third)
     wait_exchange(2)
@@ -400,8 +403,7 @@
     @pl.loop(0, rows)
     def _(r):
         here = pl.ds(r * per, per)
-        value = received(2, r) + q2_ref[here].reshape(lines, width)
-        matched = times_match(value).reshape(tile)
+        matched = received(2, r).reshape(tile)
         put_row(poheld, r, newp_ref[here] + 0.5 * step * matched)
 
     start_panels(pout_ref, poheld, 3, True)

time: 88.5 us -> 86.3 us (0.975)
  Pallas kernels: 81.6 us -> 79.4 us
    pallas_call x1, Pallas kernels: 81.6 us -> 79.4 us  [body(): pl.pallas_call(functools.partial(kernel, n), out_shape=(jax.ShapeDtypeStr...]
where the time goes in v4:
time: 86.3 us; the launch traced here: 85.1 us
  Pallas kernels  79.4 us (92%)
  local copies, waits for them, and re-layouts  4.03 us (5%)
  other arithmetic  0.99 us (1%)
    pallas_call x1, Pallas kernels, body(): pl.pallas_call(functools.partial(kernel, n), out_shape=(jax.ShapeDtypeStr...  79.4 us
    unnamed x6, local copies, waits for them, and re-layouts  4.03 us

profile of v4, /device:TPU:15, one launch (start us, length us, event | category | flops | bytes accessed | tf_op | source)
XLA Modules:
  0.0 85.1 jit_solution(522404880955258934)
XLA Ops:
  0.6 0.0 copy-start.1
  0.6 0.7 copy-done.1
  1.3 0.2 convert_reduce_fusion.1
  1.5 0.8 convert_reduce_fusion
  2.3 79.4 %shard_map.122 = (f32[128,2048]{1,0:T(8,128)}, f32[128,2048]{1,0:T(8,128)}) custom-call(s32[256]{0:T(256)} %get-tuple-element.7.order_ref, s32[256]{0:T(256)} %get-tuple-element.6.pos_ref, f32[8]{0:T(128)} %step_ref.1, s32[16,16]{1,0:T(8,128)} %kind_ref.1, f32[128,2048]{1,0:T(8,128)} %bitcast.6, f32[128,2048]{1,0:T(8,128)} %bitcast.7, f32[16,2048]{1,0:T(8,128)} %counts_in.1, ...), custom_call_target="tpu_custom_call" | custom-call | tf_op jit(solution)/shard_map/pallas_call | solution.py:448
  81.7 0.0 copy-start
  81.7 2.4 %copy.15 = f32[8,16,2048]{2,1,0:T(8,128)} copy(f32[8,16,2048]{2,1,0:T(8,128)} %bitcast.5) | data formatting | bytes 2097152
  84.1 0.0 copy-done
  84.1 1.0 %copy.16 = f32[8,16,2048]{2,1,0:T(8,128)} copy(f32[8,16,2048]{2,1,0:T(8,128)S(1)} %bitcast.4) | data formatting | bytes 2097152
  (1 shorter events, 0.0 us)
Async XLA Ops:
  0.6 0.7 copy-start.1
  81.7 2.4 %copy-start = (f32[128,2048]{1,0:T(8,128)S(1)}, f32[128,2048]{1,0:T(8,128)}, u32[]{:S(2)}) copy-start(f32[128,2048]{1,0:T(8,128)} %get-tuple-element.5) | copy-start | bytes 3145732

commit v5 on v4

--- a/solution.py
+++ b/solution.py
@@ -42,6 +42,7 @@
     newx_ref,
     newp_ref,
     half_ref,
+    wm_ref,
     w_ref,
     moved_ref,
     wfull_ref,
@@ -335,17 +336,20 @@
         here = pl.ds(r * per, per)
         half = take_row(pheld, r) - 0.5 * step * grad
         half_ref[here] = half
-        w_ref[here] = x_ref[here] + step * half
+        ahead = x_ref[here] + step * half
+        w_ref[here] = ahead
+        wm_ref[here] = times_match(ahead.reshape(lines, width)).reshape(tile)
 
     wait_panels(pin_ref, pheld, 1)
     all_rows(x_ref, 0, use_first)
-    start_exchange(w_ref, 1, 0, early)
+    start_exchange(wm_ref, 1, 0, early)
 
     @pl.loop(0, rows)
     def _(r):
         here = pl.ds(r * per, per)
         product = times_match(x_ref[here].reshape(lines, width)).reshape(tile)
-        q1_ref[here] = 0.5 * step * step * product
+        twice = (0.5 * step * step * product).reshape(lines, width)
+        q1_ref[here] = times_match(twice).reshape(tile)
 
     wait_exchange(0)
 
@@ -357,7 +361,7 @@
         moved_ref[here] = w_ref[here] + 0.5 * step * step * matched
 
     start_edges(moved_ref, 1)
-    start_exchange(w_ref, 1, early, n - 1)
+    start_exchange(wm_ref, 1, early, n - 1)
 
     def use_second(r, grad):
         here = pl.ds(r * per, per)
@@ -382,8 +386,7 @@
     @pl.loop(0, rows)
     def _(r):
         here = pl.ds(r * per, per)
-        value = received(1, r) + q1_ref[here].reshape(lines, width)
-        matched = times_match(value).reshape(tile)
+        matched = received(1, r).reshape(tile) + q1_ref[here]
         wfull_ref[here] = wfull_ref[here] + step * matched
         newx = w2_ref[here] + step * step * matched
         newx_ref[here] = newx
@@ -450,7 +453,7 @@
         out_shape=(jax.ShapeDtypeStruct(flat, f32), jax.ShapeDtypeStruct(flat, f32)),
         in_specs=[smem] * 4 + [hbm] * 8,
         out_specs=(hbm, hbm),
-        scratch_shapes=[big() for _ in range(10)]
+        scratch_shapes=[big() for _ in range(11)]
         + [
             pltpu.VMEM(((rows + 2) * lines, width), bf16),
             pltpu.VMEM(((rows + 2) * lines, width), bf16),

time: 86.3 us -> 85.9 us (level)
  no operation moved by 1% of the time
where the time goes in v5:
time: 85.9 us; the launch traced here: 85 us
  Pallas kernels  79.3 us (92%)
  local copies, waits for them, and re-layouts  4.03 us (5%)
  other arithmetic  0.99 us (1%)
    pallas_call x1, Pallas kernels, body(): pl.pallas_call(functools.partial(kernel, n), out_shape=(jax.ShapeDtypeStr...  79.3 us
    unnamed x6, local copies, waits for them, and re-layouts  4.03 us

profile of v5, /device:TPU:15, one launch (start us, length us, event | category | flops | bytes accessed | tf_op | source)
XLA Modules:
  0.0 85.0 jit_solution(7577638442726261096)
XLA Ops:
  0.6 0.0 copy-start.1
  0.6 0.7 copy-done.1
  1.3 0.2 convert_reduce_fusion.1
  1.5 0.8 convert_reduce_fusion
  2.3 79.3 %shard_map.122 = (f32[128,2048]{1,0:T(8,128)}, f32[128,2048]{1,0:T(8,128)}) custom-call(s32[256]{0:T(256)} %get-tuple-element.7.order_ref, s32[256]{0:T(256)} %get-tuple-element.6.pos_ref, f32[8]{0:T(128)} %step_ref.1, s32[16,16]{1,0:T(8,128)} %kind_ref.1, f32[128,2048]{1,0:T(8,128)} %bitcast.6, f32[128,2048]{1,0:T(8,128)} %bitcast.7, f32[16,2048]{1,0:T(8,128)} %counts_in.1, ...), custom_call_target="tpu_custom_call" | custom-call | tf_op jit(solution)/shard_map/pallas_call | solution.py:451
  81.6 0.0 copy-start
  81.7 2.4 %copy.15 = f32[8,16,2048]{2,1,0:T(8,128)} copy(f32[8,16,2048]{2,1,0:T(8,128)} %bitcast.5) | data formatting | bytes 2097152
  84.0 0.0 copy-done
  84.0 1.0 %copy.16 = f32[8,16,2048]{2,1,0:T(8,128)} copy(f32[8,16,2048]{2,1,0:T(8,128)S(1)} %bitcast.4) | data formatting | bytes 2097152
  (1 shorter events, 0.0 us)
Async XLA Ops:
  0.6 0.7 copy-start.1
  81.6 2.4 %copy-start = (f32[128,2048]{1,0:T(8,128)S(1)}, f32[128,2048]{1,0:T(8,128)}, u32[]{:S(2)}) copy-start(f32[128,2048]{1,0:T(8,128)} %get-tuple-element.5) | copy-start | bytes 3145732
